TPU v7x, 32 devices: a whole 2x2x4 slice. The times are simulated.
32 devices in a mesh: segment: 2 (over core), space: 16 (over z, y, x).
Axes of the slice: x: 2, y: 2, z: 4, core: 2. Of those that a mesh axis runs over, the one named last changes fastest.
Arguments:
- stash_down: bfloat16 [2, 64, 32, 384], P('segment', 'space'), may hold values from -6 to 6
- stash_up: bfloat16 [2, 64, 32, 384], P('segment', 'space'), may hold values from -6 to 6
- grad_down: bfloat16 [64, 32, 384], P('space'), may hold values from -6 to 6
- grad_up: bfloat16 [64, 32, 384], P('space'), may hold values from -6 to 6
- dw_kernel: bfloat16 [2, 2, 49, 384], P('segment'), as said below
- norm_gain: float32 [2, 2, 384], P('segment'), as said below
- norm_bias: float32 [2, 2, 384], P('segment'), as said below
- w_in: bfloat16 [2, 2, 384, 1536], P('segment', None, 'space'), as said below
- b_in: float32 [2, 2, 1536], P('segment'), as said below
- w_out: bfloat16 [2, 2, 1536, 384], P('segment', None, 'space'), as said below
- layer_scale: float32 [2, 2, 384], P('segment'), as said below
Outputs:
- input_grad_down: bfloat16 [2, 64, 32, 384], P('segment', 'space')
- input_grad_up: bfloat16 [2, 64, 32, 384], P('segment', 'space')
- w_out_grad: float32 [2, 1536, 384], P('segment', 'space')
- kernel_grad: float32 [2, 49, 384], P('segment')
Inputs may be any that keep to these rules, and one draw needn't show every extreme that they name: `dw_kernel`: entry [s, 1] equals entry [1 - s, 0] for every s. `norm_gain`: entry [s, 1] equals entry [1 - s, 0] for every s. `norm_bias`: entry [s, 1] equals entry [1 - s, 0] for every s. `w_in`: entry [s, 1] equals entry [1 - s, 0] for every s. `b_in`: entry [s, 1] equals entry [1 - s, 0] for every s. `w_out`: entry [s, 1] equals entry [1 - s, 0] for every s. `layer_scale`: entry [s, 1] equals entry [1 - s, 0] for every s.
All inputs are finite; a program needn't handle non-finite values.
Results may differ from a plain program's by a relative error of at most 0.0075.
Values may be sent and summed in bfloat16 or wider, within the bound.
A program may use at most 64 MiB of HBM per device.

v0:
```python
import math
import jax
import jax.numpy as jnp
from jax import lax
from jax.sharding import PartitionSpec as P

KSIDE = 7


def padded_2(cells, sides, width):
    for axis, dim in sides:
        count = lax.axis_size(axis)
        ends = count - 1
        head = lax.slice_in_dim(cells, 0, width, axis=dim)
        tail = lax.slice_in_dim(cells, cells.shape[dim] - width, cells.shape[dim], axis=dim)
        cells = jnp.concatenate(
            [
                lax.ppermute(tail, axis, [(i, (i + 1) % count) for i in range(ends)]),
                cells,
                lax.ppermute(head, axis, [((i + 1) % count, i) for i in range(ends)]),
            ],
            axis=dim,
        )
    return cells


def passed_along(shard, axis, by):
    devices = lax.axis_size(axis)
    pairs = [(i, i + by) for i in range(devices) if 0 <= i + by < devices]
    return lax.ppermute(shard, axis, pairs)


def as_sent(shard):
    return jax.tree.map(lambda a: a.astype(jnp.bfloat16) if a.dtype == jnp.float32 else a, shard)


def swapped(block, axis, stride):
    count = lax.axis_size(axis)
    route = []
    for low in range(count):
        high = low | 1 << stride
        if high != low and high < count:
            route += [(low, high), (high, low)]
    return lax.ppermute(block, axis, route)


def gelu_parts(a):
    inner = 0.7978845608 * (a + 0.044715 * a * a * a)
    th = jnp.tanh(inner)
    value = 0.5 * a * (1.0 + th)
    slope = 0.5 * (1.0 + th) + 0.5 * a * (1.0 - th * th) * 0.7978845608 * (1.0 + 0.134145 * a * a)
    return (value, slope)


def grouped_conv(padded, filters):
    chans = padded.shape[2]
    result = lax.conv_general_dilated(
        padded[None],
        filters,
        (1, 1),
        "VALID",
        dimension_numbers=("NHWC", "HWIO", "NHWC"),
        feature_group_count=chans,
        precision=lax.Precision.HIGHEST,
    )
    return result[0]


def depthwise(padded, kernel):
    chans = kernel.shape[1]
    filters = kernel.reshape(KSIDE, KSIDE, 1, chans)
    return grouped_conv(padded, filters)


def depthwise_back(padded, kernel):
    chans = kernel.shape[1]
    filters = kernel.reshape(KSIDE, KSIDE, 1, chans)[::-1, ::-1]
    return grouped_conv(padded, filters)


def kernel_terms(padded, grad):
    rows, cols, chans = grad.shape
    filters = grad.reshape(rows, cols, 1, chans)
    return grouped_conv(padded, filters).reshape(KSIDE * KSIDE, chans)


def pointwise_back(v, g, gain, bias, w_first, b_first, w_second, scale_res):
    rows, cols, chans = v.shape
    flat = v.reshape(rows * cols, chans)
    mean_v = jnp.mean(flat, axis=1, keepdims=True)
    centred = flat - mean_v
    rs = lax.rsqrt(jnp.mean(centred * centred, axis=1, keepdims=True) + 1e-06)
    nh = centred * rs
    normed = (nh * gain + bias).astype(jnp.bfloat16)
    pre = jnp.dot(normed, w_first, preferred_element_type=jnp.float32) + b_first
    value, slope = gelu_parts(pre)
    hidden = value.astype(jnp.bfloat16)
    outer = (g.reshape(rows * cols, chans).astype(jnp.float32) * scale_res).astype(jnp.bfloat16)
    dh = lax.dot_general(
        outer, w_second, (((1,), (1,)), ((), ())), preferred_element_type=jnp.float32
    )
    da = (dh * slope).astype(jnp.bfloat16)
    dn = lax.dot_general(da, w_first, (((1,), (1,)), ((), ())), preferred_element_type=jnp.float32)
    q = dn * gain
    du = rs * (
        q - jnp.mean(q, axis=1, keepdims=True) - nh * jnp.mean(q * nh, axis=1, keepdims=True)
    )
    return (du.astype(jnp.bfloat16).reshape(rows, cols, chans), hidden, outer)


def per_device(
    stash_down,
    stash_up,
    grad_down,
    grad_up,
    dw_kernel,
    norm_gain,
    norm_bias,
    w_in,
    b_in,
    w_out,
    layer_scale,
):
    segments = lax.axis_size("segment")
    me = lax.axis_index("segment")
    half = KSIDE // 2
    rows, cols, chans = (stash_down.shape[1], stash_down.shape[2], stash_down.shape[3])
    hidden_units = w_in.shape[3]
    norm = 1.0 / math.sqrt(2.0 * rows * lax.axis_size("space") * cols)
    w_in_all, w_out_all = (
        lax.all_gather(w_in, "space", axis=2, tiled=True),
        lax.all_gather(w_out, "space", axis=2, tiled=True),
    )
    x_down = stash_down[0]
    x_up = stash_up[0]
    rimmed_both = padded_2(jnp.stack([x_down, x_up]), (("space", 1),), half)
    down_in = grad_down
    up_in = grad_up
    out_down = jnp.zeros_like(grad_down)
    out_up = jnp.zeros_like(grad_up)
    tokens = rows * cols
    hid_down = jnp.zeros((tokens, hidden_units), jnp.bfloat16)
    hid_up = jnp.zeros((tokens, hidden_units), jnp.bfloat16)
    outer_down = jnp.zeros((tokens, chans), jnp.bfloat16)
    outer_up = jnp.zeros((tokens, chans), jnp.bfloat16)
    kern_down = jnp.zeros((KSIDE * KSIDE, chans), jnp.float32)
    kern_up = jnp.zeros((KSIDE * KSIDE, chans), jnp.float32)
    for step in range(segments):
        on_up = me == step
        on_down = me == segments - 1 - step
        active = jnp.logical_or(on_up, on_down)
        pick = on_up.astype(jnp.int32)

        def select(array):
            return lax.dynamic_index_in_dim(array[0], pick, 0, keepdims=False)

        rimmed = jnp.where(on_up, rimmed_both[1], rimmed_both[0])
        padded = jnp.pad(rimmed.astype(jnp.float32), ((0, 0), (half, half), (0, 0)))
        g = jnp.where(on_up, up_in, down_in)
        kern = select(dw_kernel).astype(jnp.float32)

        def front_live():
            v = depthwise(padded, kern)
            return pointwise_back(
                v,
                g,
                select(norm_gain),
                select(norm_bias),
                select(w_in_all),
                select(b_in),
                select(w_out_all),
                select(layer_scale),
            )

        def front_spare():
            return (
                jnp.zeros((rows, cols, chans), jnp.bfloat16),
                jnp.zeros((tokens, hidden_units), jnp.bfloat16),
                jnp.zeros((tokens, chans), jnp.bfloat16),
            )

        du, hidden, outer = lax.cond(active, front_live, front_spare)
        du_rimmed = padded_2(du, (("space", 0),), half)

        def back_live():
            du_pad = jnp.pad(du_rimmed.astype(jnp.float32), ((0, 0), (half, half), (0, 0)))
            dx_new = (g.astype(jnp.float32) + depthwise_back(du_pad, kern)).astype(jnp.bfloat16)
            dk_new = kernel_terms(padded, du.astype(jnp.float32))
            return (dx_new, dk_new)

        def back_spare():
            return (
                jnp.zeros((rows, cols, chans), jnp.bfloat16),
                jnp.zeros((KSIDE * KSIDE, chans), jnp.float32),
            )

        dx, dk = lax.cond(active, back_live, back_spare)
        out_down = jnp.where(on_down, dx, out_down)
        out_up = jnp.where(on_up, dx, out_up)
        kern_down = jnp.where(on_down, dk, kern_down)
        kern_up = jnp.where(on_up, dk, kern_up)
        hid_down = jnp.where(on_down, hidden, hid_down)
        hid_up = jnp.where(on_up, hidden, hid_up)
        outer_down = jnp.where(on_down, outer, outer_down)
        outer_up = jnp.where(on_up, outer, outer_up)
        if step + 1 < segments:
            down_in = passed_along(dx, "segment", -1)
            up_in = passed_along(dx, "segment", 1)
    levels = segments.bit_length() - 1
    for bit in range(levels):
        kern_up = swapped(as_sent(kern_up), "segment", bit).astype(kern_up.dtype)
    share = w_out.shape[2]
    joined = jnp.concatenate([hid_up, outer_up], axis=1)
    for bit in range(levels):
        joined = swapped(joined, "segment", bit)
    all_hidden = jnp.concatenate([hid_down, joined[:, :hidden_units]], axis=0)
    all_outer = jnp.concatenate([outer_down, joined[:, hidden_units:]], axis=0)
    columns = lax.slice_in_dim(all_hidden, 0, share * lax.axis_size("space"), axis=1)
    w_grad = lax.psum_scatter(
        lax.dot_general(
            columns, all_outer, (((0,), (0,)), ((), ())), preferred_element_type=jnp.float32
        )
        * norm,
        "space",
        scatter_dimension=0,
        tiled=True,
    )
    k_grad = lax.psum(kern_down + kern_up, "space") * norm
    return (out_down[None], out_up[None], w_grad[None], k_grad[None])


def solution(mesh):
    return jax.shard_map(
        per_device,
        mesh=mesh,
        in_specs=(
            P("segment", "space", None, None),
            P("segment", "space", None, None),
            P("space", None, None),
            P("space", None, None),
            P("segment", None, None, None),
            P("segment", None, None),
            P("segment", None, None),
            P("segment", None, "space", None),
            P("segment", None, None),
            P("segment", None, "space", None),
            P("segment", None, None),
        ),
        out_specs=(
            P("segment", "space", None, None),
            P("segment", "space", None, None),
            P("segment", "space", None),
            P("segment", None, None),
        ),
        check_vma=False,
    )
```

profile of v0, /device:TPU:0, one launch (start us, length us, event | category | flops | bytes accessed | tf_op | source)
XLA Modules:
  0.0 438.8 jit_solution(5692250722293077002)
XLA Ops:
  11.9 5.5 %collective-permute-start = (bf16[2,3,32,384]{3,2,1,0:T(8,128)(2,1)S(1)}, bf16[2,3,32,384]{3,2,1,0:T(8,128)(2,1)S(1)}, u32[]{:S(2)}, u32[]{:S(2)}) collective-permute-start(bf16[2,3,32,384]{3,2,1,0:T(8,128)(2,1)S(1)} %get-tuple-element.140), channel_id=1, source_target_pairs={{0,1},{1,2},{2,3},{3,4},{4,5},{5,6},{6,7},{7,8},{8,9},{9,10},{10,1... | collective-permute-start | bytes 442376 | tf_op jit(solution)/shard_map/ppermute | solution.py:18
  19.5 5.1 %collective-permute-done = bf16[2,3,32,384]{3,2,1,0:T(8,128)(2,1)S(1)} collective-permute-done((bf16[2,3,32,384]{3,2,1,0:T(8,128)(2,1)S(1)}, bf16[2,3,32,384]{3,2,1,0:T(8,128)(2,1)S(1)}, u32[]{:S(2)}, u32[]{:S(2)}) %collective-permute-start) | collective-permute-done | bytes 147488 | tf_op jit(solution)/shard_map/ppermute | solution.py:18
  24.8 51.0 %all-gather.3.cloned.1.call-done = bf16[1,2,1536,384]{3,2,1,0:T(8,128)(2,1)} async-done(((bf16[1,2,96,384]{3,2,1,0:T(8,128)(2,1)}), bf16[1,2,1536,384]{3,2,1,0:T(8,128)(2,1)}) %all-gather.3.cloned.1.call-update) | async-done | bytes 2359312 | tf_op jit(solution)/shard_map/all_gather | solution.py:132
  75.8 63.9 %all-gather.5.cloned.1.call-done = bf16[1,2,384,1536]{3,2,1,0:T(8,128)(2,1)} async-done(((bf16[1,2,24,1536]{3,2,1,0:T(8,128)(2,1)}), bf16[1,2,384,1536]{3,2,1,0:T(8,128)(2,1)}) %all-gather.5.cloned.1.call-update) | async-done | bytes 2359312 | tf_op jit(solution)/shard_map/all_gather | solution.py:131
  139.7 10.4 %conditional.4 = (bf16[4,32,384]{2,1,0:T(8,128)(2,1)S(1)}, bf16[128,1536]{1,0:T(8,128)(2,1)S(1)}, bf16[128,384]{1,0:T(8,128)(2,1)S(1)}) conditional(s32[]{:T(128)} %convert_element_type.123, () %tuple.42, (f32[10,38,384]{2,1,0:T(8,128)S(1)}, f32[49,384]{1,0:T(8,128)S(1)}, bf16[4,32,384]{2,1,0:T(8,128)(2,1)S(1)}, s32[]{:T(128)}, ...), branch_computations={%region_0.1_spmd, %region_1.6_spmd} | conditional | flops 488964224 | bytes 9116234 | solution.py:182
  139.8 4.1 fusion.113
  145.5 1.8 multiply_convert_fusion
  147.3 2.6 fusion.111
  151.4 4.5 %collective-permute-start.2 = (bf16[3,32,384]{2,1,0:T(8,128)(2,1)S(1)}, bf16[3,32,384]{2,1,0:T(8,128)(2,1)S(1)}, u32[]{:S(2)}, u32[]{:S(2)}) collective-permute-start(bf16[3,32,384]{2,1,0:T(8,128)(2,1)S(1)} %get-tuple-element.144), channel_id=1, source_target_pairs={{0,1},{1,2},{2,3},{3,4},{4,5},{5,6},{6,7},{7,8},{8,9},{9,10},{10,1... | collective-permute-start | bytes 221192 | tf_op jit(solution)/shard_map/ppermute | solution.py:18
  158.0 4.3 conditional.5
  158.2 1.8 fusion.47
  160.0 2.3 convolution_reduce_fusion
  164.9 1.8 collective-permute-done.5
  166.8 10.4 %conditional.6 = (bf16[4,32,384]{2,1,0:T(8,128)(2,1)S(1)}, bf16[128,1536]{1,0:T(8,128)(2,1)S(1)}, bf16[128,384]{1,0:T(8,128)(2,1)S(1)}) conditional(s32[]{:T(128)} %convert_element_type.123, () %tuple.45, (f32[10,38,384]{2,1,0:T(8,128)S(1)}, f32[49,384]{1,0:T(8,128)S(1)}, bf16[4,32,384]{2,1,0:T(8,128)(2,1)S(1)}, s32[]{:T(128)}, ...), branch_computations={%region_8.9_spmd, %region_9.14_spmd} | conditional | flops 488964224 | bytes 9116234 | solution.py:182
  166.9 4.1 fusion.116
  174.4 2.6 fusion.112
  178.5 4.9 %collective-permute-start.6 = (bf16[3,32,384]{2,1,0:T(8,128)(2,1)S(1)}, bf16[3,32,384]{2,1,0:T(8,128)(2,1)S(1)}, u32[]{:S(2)}, u32[]{:S(2)}) collective-permute-start(bf16[3,32,384]{2,1,0:T(8,128)(2,1)S(1)} %get-tuple-element.142), channel_id=1, source_target_pairs={{0,1},{1,2},{2,3},{3,4},{4,5},{5,6},{6,7},{7,8},{8,9},{9,10},{10,1... | collective-permute-start | bytes 221192 | tf_op jit(solution)/shard_map/ppermute | solution.py:18
  184.1 2.8 collective-permute-done.6
  186.9 4.3 conditional.7
  187.1 1.8 fusion.98
  188.9 2.2 convolution_reduce_fusion.1
  193.2 2.0 convolution_multiply_fusion.2
  196.0 103.2 %all-reduce.6.cloned.1.call-done = f32[49,384]{1,0:T(8,128)} async-done(((f32[49,384]{1,0:T(8,128)}), f32[49,384]{1,0:T(8,128)}) %all-reduce.6.cloned.1.call-update) | async-done | bytes 75280 | tf_op jit(solution)/shard_map/psum | solution.py:228
  300.8 131.5 %reduce-scatter.2.cloned.1.call-done = f32[96,384]{1,0:T(8,128)} async-done(((f32[1536,384]{1,0:T(8,128)}), f32[96,384]{1,0:T(8,128)}) %reduce-scatter.2.cloned.1.call-update) | async-done | bytes 147472 | tf_op jit(solution)/shard_map/reduce_scatter | solution.py:219
  (99 shorter events, 24.9 us)
Async XLA Ops:
  7.2 68.6 %all-gather.3.cloned.1.call-start = ((), (), s32[]{:S(2)}) async-start(), calls=%async_computation.1 | async-start | bytes 2506752 | tf_op jit(solution)/shard_map/all_gather | solution.py:132
  7.9 131.8 %copy-start = (f32[1,2,1536]{2,1,0:T(2,128)S(1)}, f32[1,2,1536]{2,1,0:T(2,128)}, u32[]{:S(2)}) copy-start(f32[1,2,1536]{2,1,0:T(2,128)} %param.27) | copy-start | bytes 36868
  7.9 131.8 %copy-start.1 = (f32[1,2,384]{2,1,0:T(2,128)S(1)}, f32[1,2,384]{2,1,0:T(2,128)}, u32[]{:S(2)}) copy-start(f32[1,2,384]{2,1,0:T(2,128)} %param.29) | copy-start | bytes 9220
  7.9 131.7 %copy-start.2 = (f32[1,2,384]{2,1,0:T(2,128)S(1)}, f32[1,2,384]{2,1,0:T(2,128)}, u32[]{:S(2)}) copy-start(f32[1,2,384]{2,1,0:T(2,128)} %param.24) | copy-start | bytes 9220
  7.9 131.7 %copy-start.3 = (f32[1,2,384]{2,1,0:T(2,128)S(1)}, f32[1,2,384]{2,1,0:T(2,128)}, u32[]{:S(2)}) copy-start(f32[1,2,384]{2,1,0:T(2,128)} %param.25) | copy-start | bytes 9220
  7.9 131.7 %all-gather.5.cloned.1.call-start = ((), (), s32[]{:S(2)}) async-start(), calls=%async_computation.2 | async-start | bytes 2506752 | tf_op jit(solution)/shard_map/all_gather | solution.py:131
  8.7 290.5 %all-reduce.6.cloned.1.call-start = ((), (), s32[]{:S(2)}) async-start(), calls=%async_computation.4 | async-start | bytes 172032 | tf_op jit(solution)/shard_map/psum | solution.py:228
  10.6 8.9 %collective-permute-start.1 = (bf16[2,3,32,384]{3,2,1,0:T(8,128)(2,1)S(1)}, bf16[2,3,32,384]{3,2,1,0:T(8,128)(2,1)S(1)}, u32[]{:S(2)}, u32[]{:S(2)}) collective-permute-start(bf16[2,3,32,384]{3,2,1,0:T(8,128)(2,1)S(1)} %get-tuple-element.141), channel_id=1, source_target_pairs={{1,0},{2,1},{3,2},{4,3},{5,4},{6,5},{7,6},{8,7},{9,8},{10,9},{11,1... | collective-permute-start | bytes 442376 | tf_op jit(solution)/shard_map/ppermute | solution.py:20
  11.9 12.7 %collective-permute-start = (bf16[2,3,32,384]{3,2,1,0:T(8,128)(2,1)S(1)}, bf16[2,3,32,384]{3,2,1,0:T(8,128)(2,1)S(1)}, u32[]{:S(2)}, u32[]{:S(2)}) collective-permute-start(bf16[2,3,32,384]{3,2,1,0:T(8,128)(2,1)S(1)} %get-tuple-element.140), channel_id=1, source_target_pairs={{0,1},{1,2},{2,3},{3,4},{4,5},{5,6},{6,7},{7,8},{8,9},{9,10},{10,1... | collective-permute-start | bytes 442376 | tf_op jit(solution)/shard_map/ppermute | solution.py:18
  150.1 6.2 %collective-permute-start.3 = (bf16[3,32,384]{2,1,0:T(8,128)(2,1)S(1)}, bf16[3,32,384]{2,1,0:T(8,128)(2,1)S(1)}, u32[]{:S(2)}, u32[]{:S(2)}) collective-permute-start(bf16[3,32,384]{2,1,0:T(8,128)(2,1)S(1)} %get-tuple-element.145), channel_id=1, source_target_pairs={{1,0},{2,1},{3,2},{4,3},{5,4},{6,5},{7,6},{8,7},{9,8},{10,9},{11,1... | collective-permute-start | bytes 221192 | tf_op jit(solution)/shard_map/ppermute | solution.py:20
  151.4 6.5 %collective-permute-start.2 = (bf16[3,32,384]{2,1,0:T(8,128)(2,1)S(1)}, bf16[3,32,384]{2,1,0:T(8,128)(2,1)S(1)}, u32[]{:S(2)}, u32[]{:S(2)}) collective-permute-start(bf16[3,32,384]{2,1,0:T(8,128)(2,1)S(1)} %get-tuple-element.144), channel_id=1, source_target_pairs={{0,1},{1,2},{2,3},{3,4},{4,5},{5,6},{6,7},{7,8},{8,9},{9,10},{10,1... | collective-permute-start | bytes 221192 | tf_op jit(solution)/shard_map/ppermute | solution.py:18
  162.3 2.7 collective-permute-start.4
  163.6 3.2 collective-permute-start.5
  177.2 6.9 %collective-permute-start.7 = (bf16[3,32,384]{2,1,0:T(8,128)(2,1)S(1)}, bf16[3,32,384]{2,1,0:T(8,128)(2,1)S(1)}, u32[]{:S(2)}, u32[]{:S(2)}) collective-permute-start(bf16[3,32,384]{2,1,0:T(8,128)(2,1)S(1)} %get-tuple-element.143), channel_id=1, source_target_pairs={{1,0},{2,1},{3,2},{4,3},{5,4},{6,5},{7,6},{8,7},{9,8},{10,9},{11,1... | collective-permute-start | bytes 221192 | tf_op jit(solution)/shard_map/ppermute | solution.py:20
  178.5 8.3 %collective-permute-start.6 = (bf16[3,32,384]{2,1,0:T(8,128)(2,1)S(1)}, bf16[3,32,384]{2,1,0:T(8,128)(2,1)S(1)}, u32[]{:S(2)}, u32[]{:S(2)}) collective-permute-start(bf16[3,32,384]{2,1,0:T(8,128)(2,1)S(1)} %get-tuple-element.142), channel_id=1, source_target_pairs={{0,1},{1,2},{2,3},{3,4},{4,5},{5,6},{6,7},{7,8},{8,9},{9,10},{10,1... | collective-permute-start | bytes 221192 | tf_op jit(solution)/shard_map/ppermute | solution.py:18
  183.6 9.6 %collective-permute-start.8 = (bf16[128,1920]{1,0:T(8,128)(2,1)S(1)}, bf16[128,1920]{1,0:T(8,128)(2,1)S(1)}, u32[]{:S(2)}, u32[]{:S(2)}) collective-permute-start(bf16[128,1920]{1,0:T(8,128)(2,1)S(1)} %pad_maximum_fusion.1), channel_id=1, source_target_pairs={{0,16},{16,0},{1,17},{17,1},{2,18},{18,2},{3,19},{19,3},{4,20},{20... | collective-permute-start | bytes 1474568 | tf_op jit(solution)/shard_map/ppermute | solution.py:44
  191.2 1.3 collective-permute-start.9
  193.1 239.2 %reduce-scatter.2.cloned.1.call-start = ((), (), s32[]{:S(2)}) async-start(), calls=%async_computation.3 | async-start | bytes 2506752 | tf_op jit(solution)/shard_map/reduce_scatter | solution.py:219
Sparse Core Ops, SparseCore 0:
  10.7 65.0 all-gather.2
  78.5 61.1 all-gather.4
  193.2 105.9 all-reduce.5
  304.5 127.6 reduce-scatter.1
where the time goes:
time: 439 us
  waiting for transfers between devices  364 us (83%)
  matrix products  27 us (6%)
  starting transfers between devices  21.7 us (5%)
  between operations  14.1 us (3%)
  other arithmetic  6.63 us (2%)
  local copies, waits for them, and re-layouts  4.77 us (1%)
    reduce_scatter x1, waiting for transfers between devices, per_device(): lax.psum_scatter(lax.dot_general(columns, all_outer, (((0,), (0,)), ((),...  131 us
    psum x1, waiting for transfers between devices, per_device(): k_grad = lax.psum(kern_down + kern_up, 'space') * norm  103 us
    all_gather x1, waiting for transfers between devices, per_device(): lax.all_gather(w_in, 'space', axis=2, tiled=True)  63.9 us
    all_gather x1, waiting for transfers between devices, per_device(): lax.all_gather(w_out, 'space', axis=2, tiled=True)  51 us
    conv_general_dilated x6, matrix products, grouped_conv(): lax.conv_general_dilated(padded[None], filters, (1, 1), 'VALID', dimensio...  16.2 us
    ppermute x3, starting transfers between devices, padded_2(): lax.ppermute(tail, axis, [(i, (i + 1) % count) for i in range(ends)])  14.9 us
    ppermute x3, waiting for transfers between devices, padded_2(): lax.ppermute(tail, axis, [(i, (i + 1) % count) for i in range(ends)])  9.47 us
  transfers between devices with their start and end apart: 14, of which 11 were waited for; matrix products, arithmetic and copies ran while one was open for 3% of the time, Pallas kernels for 0%

commit v1 on v0

--- a/solution.py
+++ b/solution.py
@@ -5,6 +5,24 @@
 from jax.sharding import PartitionSpec as P
 
 KSIDE = 7
+
+
+def gather_around(value, axis, dim):
+    ways, here, step = (lax.axis_size(axis), lax.axis_index(axis), value.shape[dim])
+    dims = [n * ways if d == dim else n for d, n in enumerate(value.shape)]
+    full = lax.dynamic_update_slice_in_dim(
+        jnp.zeros(dims, value.dtype), value, here * step, axis=dim
+    )
+    going_up = going_down = value
+    for far in range(1, ways // 2 + 1):
+        going_up = lax.ppermute(going_up, axis, [(d, (d + 1) % ways) for d in range(ways)])
+        full = lax.dynamic_update_slice_in_dim(full, going_up, (here - far) % ways * step, axis=dim)
+        if 2 * far < ways:
+            going_down = lax.ppermute(going_down, axis, [(d, (d - 1) % ways) for d in range(ways)])
+            full = lax.dynamic_update_slice_in_dim(
+                full, going_down, (here + far) % ways * step, axis=dim
+            )
+    return full
 
 
 def padded_2(cells, sides, width):
@@ -128,7 +146,7 @@
     hidden_units = w_in.shape[3]
     norm = 1.0 / math.sqrt(2.0 * rows * lax.axis_size("space") * cols)
     w_in_all, w_out_all = (
-        lax.all_gather(w_in, "space", axis=2, tiled=True),
+        gather_around(w_in, "space", 2),
         lax.all_gather(w_out, "space", axis=2, tiled=True),
     )
     x_down = stash_down[0]

time: 439 us -> 400 us (0.911)
  waiting for transfers between devices: 364 us -> 277 us
  starting transfers between devices: 21.7 us -> 59.2 us
  other arithmetic: 6.63 us -> 13.2 us
    all_gather x1 -> x0, waiting for transfers between devices: 63.9 us -> none  [per_device(): lax.all_gather(w_in, 'space', axis=2, tiled=True)]
    all_gather x1, waiting for transfers between devices: 51 us -> 2.59 us  [per_device(): lax.all_gather(w_out, 'space', axis=2, tiled=True)]
    ppermute x0 -> x15, starting transfers between devices: none -> 42.8 us  [the longest x7 33.3 us: gather_around(): lax.ppermute(going_down, axis, [(d, (d - 1) % ways) for d in range(ways)])]
    ppermute x0 -> x15, waiting for transfers between devices: none -> 32.4 us  [the longest x8 29.2 us: gather_around(): lax.ppermute(going_up, axis, [(d, (d + 1) % ways) for d in range(ways)])]
    ppermute x3, waiting for transfers between devices: 9.47 us -> 0.01 us  [padded_2(): lax.ppermute(tail, axis, [(i, (i + 1) % count) for i in range(ends)])]
    ppermute x3, waiting for transfers between devices: 0.79 us -> 7.88 us  [padded_2(): lax.ppermute(head, axis, [((i + 1) % count, i) for i in range(ends)])]
    ppermute x3, starting transfers between devices: 14.9 us -> 9.69 us  [padded_2(): lax.ppermute(tail, axis, [(i, (i + 1) % count) for i in range(ends)])]
  transfers between devices with their start and end apart: 14 -> 28, of which waited for: 11 -> 17; matrix products, arithmetic and copies ran while one was open for 3% -> 5% of each run, Pallas kernels for 0% -> 0%
where the time goes in v1:
time: 400 us; the launch traced here: 399 us
  waiting for transfers between devices  277 us (69%)
  starting transfers between devices  59.2 us (15%)
  matrix products  26.6 us (7%)
  between operations  14.3 us (4%)
  other arithmetic  13.2 us (3%)
  local copies, waits for them, and re-layouts  8.8 us (2%)
    reduce_scatter x1, waiting for transfers between devices, per_device(): lax.psum_scatter(lax.dot_general(columns, all_outer, (((0,), (0,)), ((),...  131 us
    psum x1, waiting for transfers between devices, per_device(): k_grad = lax.psum(kern_down + kern_up, 'space') * norm  100 us
    ppermute x7, starting transfers between devices, gather_around(): lax.ppermute(going_down, axis, [(d, (d - 1) % ways) for d in range(ways)])  33.3 us
    ppermute x8, waiting for transfers between devices, gather_around(): lax.ppermute(going_up, axis, [(d, (d + 1) % ways) for d in range(ways)])  29.2 us
    conv_general_dilated x6, matrix products, grouped_conv(): lax.conv_general_dilated(padded[None], filters, (1, 1), 'VALID', dimensio...  15.6 us
    ppermute x3, starting transfers between devices, padded_2(): lax.ppermute(tail, axis, [(i, (i + 1) % count) for i in range(ends)])  9.69 us
    ppermute x8, starting transfers between devices, gather_around(): lax.ppermute(going_up, axis, [(d, (d + 1) % ways) for d in range(ways)])  9.42 us
  transfers between devices with their start and end apart: 28, of which 17 were waited for; matrix products, arithmetic and copies ran while one was open for 5% of the time, Pallas kernels for 0%

profile of v1, /device:TPU:0, one launch (start us, length us, event | category | flops | bytes accessed | tf_op | source)
XLA Modules:
  0.0 399.3 jit_solution(13067269239079098653)
XLA Ops:
  10.2 4.1 %collective-permute-start.3 = (bf16[1,2,24,1536]{3,2,1,0:T(8,128)(2,1)}, bf16[1,2,24,1536]{3,2,1,0:T(8,128)(2,1)S(1)}, u32[]{:S(2)}, u32[]{:S(2)}) collective-permute-start(bf16[1,2,24,1536]{3,2,1,0:T(8,128)(2,1)} %param.26), channel_id=1, source_target_pairs={{0,15},{1,0},{2,1},{3,2},{4,3},{5,4},{6,5},{7,6},{8,7},{9,8},{10,9... | collective-permute-start | bytes 442376 | tf_op jit(solution)/shard_map/ppermute | solution.py:21
  23.3 3.3 collective-permute-start.5
  29.6 3.9 collective-permute-done.4
  35.8 3.2 collective-permute-start.7
  39.1 3.9 collective-permute-done.6
  44.3 4.3 %collective-permute-start.9 = (bf16[1,2,24,1536]{3,2,1,0:T(8,128)(2,1)S(1)}, bf16[1,2,24,1536]{3,2,1,0:T(8,128)(2,1)S(1)}, u32[]{:S(2)}, u32[]{:S(2)}) collective-permute-start(bf16[1,2,24,1536]{3,2,1,0:T(8,128)(2,1)S(1)} %collective-permute-done.7), channel_id=1, source_target_pairs={{0,15},{1,0},{2,1},{3,2},{4,3},{5,4},{6,5},{7,6},{8,7},{9,8},{10,9... | collective-permute-start | bytes 442376 | tf_op jit(solution)/shard_map/ppermute | solution.py:21
  48.6 3.3 collective-permute-done.8
  52.1 6.2 %collective-permute-start.11 = (bf16[1,2,24,1536]{3,2,1,0:T(8,128)(2,1)S(1)}, bf16[1,2,24,1536]{3,2,1,0:T(8,128)(2,1)S(1)}, u32[]{:S(2)}, u32[]{:S(2)}) collective-permute-start(bf16[1,2,24,1536]{3,2,1,0:T(8,128)(2,1)S(1)} %collective-permute-done.9), channel_id=1, source_target_pairs={{0,15},{1,0},{2,1},{3,2},{4,3},{5,4},{6,5},{7,6},{8,7},{9,8},{10,9... | collective-permute-start | bytes 442376 | tf_op jit(solution)/shard_map/ppermute | solution.py:21
  62.8 6.0 %collective-permute-start.13 = (bf16[1,2,24,1536]{3,2,1,0:T(8,128)(2,1)S(1)}, bf16[1,2,24,1536]{3,2,1,0:T(8,128)(2,1)S(1)}, u32[]{:S(2)}, u32[]{:S(2)}) collective-permute-start(bf16[1,2,24,1536]{3,2,1,0:T(8,128)(2,1)S(1)} %collective-permute-done.11), channel_id=1, source_target_pairs={{0,15},{1,0},{2,1},{3,2},{4,3},{5,4},{6,5},{7,6},{8,7},{9,8},{10,9... | collective-permute-start | bytes 442376 | tf_op jit(solution)/shard_map/ppermute | solution.py:21
  71.5 6.2 %collective-permute-start.15 = (bf16[1,2,24,1536]{3,2,1,0:T(8,128)(2,1)S(1)}, bf16[1,2,24,1536]{3,2,1,0:T(8,128)(2,1)S(1)}, u32[]{:S(2)}, u32[]{:S(2)}) collective-permute-start(bf16[1,2,24,1536]{3,2,1,0:T(8,128)(2,1)S(1)} %collective-permute-done.13), channel_id=1, source_target_pairs={{0,15},{1,0},{2,1},{3,2},{4,3},{5,4},{6,5},{7,6},{8,7},{9,8},{10,9... | collective-permute-start | bytes 442376 | tf_op jit(solution)/shard_map/ppermute | solution.py:21
  77.8 4.3 %collective-permute-done.14 = bf16[1,2,24,1536]{3,2,1,0:T(8,128)(2,1)S(1)} collective-permute-done((bf16[1,2,24,1536]{3,2,1,0:T(8,128)(2,1)S(1)}, bf16[1,2,24,1536]{3,2,1,0:T(8,128)(2,1)S(1)}, u32[]{:S(2)}, u32[]{:S(2)}) %collective-permute-start.14) | collective-permute-done | bytes 147488 | tf_op jit(solution)/shard_map/ppermute | solution.py:18
  82.1 9.9 %collective-permute-done.16 = bf16[1,2,24,1536]{3,2,1,0:T(8,128)(2,1)S(1)} collective-permute-done((bf16[1,2,24,1536]{3,2,1,0:T(8,128)(2,1)S(1)}, bf16[1,2,24,1536]{3,2,1,0:T(8,128)(2,1)S(1)}, u32[]{:S(2)}, u32[]{:S(2)}) %collective-permute-start.16) | collective-permute-done | bytes 147488 | tf_op jit(solution)/shard_map/ppermute | solution.py:18
  94.6 11.3 %conditional.4 = (bf16[4,32,384]{2,1,0:T(8,128)(2,1)S(1)}, bf16[128,1536]{1,0:T(8,128)(2,1)S(1)}, bf16[128,384]{1,0:T(8,128)(2,1)S(1)}) conditional(s32[]{:T(128)} %convert_element_type.123, () %tuple.42, (f32[10,38,384]{2,1,0:T(8,128)}, f32[49,384]{1,0:T(8,128)S(1)}, bf16[4,32,384]{2,1,0:T(8,128)(2,1)S(1)}, s32[]{:T(128)}, ...), branch_computations={%region_0.1_spmd, %region_1.6_spmd} | conditional | flops 488964224 | bytes 9118794 | solution.py:200
  94.7 3.3 fusion.113
  105.9 4.4 %collective-permute-start.17 = (bf16[3,32,384]{2,1,0:T(8,128)(2,1)S(1)}, bf16[3,32,384]{2,1,0:T(8,128)(2,1)S(1)}, u32[]{:S(2)}, u32[]{:S(2)}) collective-permute-start(bf16[3,32,384]{2,1,0:T(8,128)(2,1)S(1)} %get-tuple-element.144), channel_id=1, source_target_pairs={{0,1},{1,2},{2,3},{3,4},{4,5},{5,6},{6,7},{7,8},{8,9},{9,10},{10,1... | collective-permute-start | bytes 221192 | tf_op jit(solution)/shard_map/ppermute | solution.py:36
  112.5 4.0 %collective-permute-done.18 = bf16[3,32,384]{2,1,0:T(8,128)(2,1)S(1)} collective-permute-done((bf16[3,32,384]{2,1,0:T(8,128)(2,1)S(1)}, bf16[3,32,384]{2,1,0:T(8,128)(2,1)S(1)}, u32[]{:S(2)}, u32[]{:S(2)}) %collective-permute-start.18) | collective-permute-done | bytes 73760 | tf_op jit(solution)/shard_map/ppermute | solution.py:38
  116.6 6.8 %conditional.5 = (bf16[4,32,384]{2,1,0:T(8,128)(2,1)S(1)}, f32[49,384]{1,0:T(8,128)S(1)}) conditional(s32[]{:T(128)} %convert_element_type.123, () %tuple.41, (bf16[4,32,384]{2,1,0:T(8,128)(2,1)S(1)}, bf16[10,32,384]{2,1,0:T(8,128)(2,1)S(1)}, f32[49,384]{1,0:T(8,128)}, f32[10,38,384]{2,1,0:T(8,128)}, bf16[4,32,384]{2,1,0:T(8,128)(2,1)S(1)}) %tuple.81), branch_computations={%region_6.7_spmd, %region_7.8_spmd} | conditional | flops 57950208 | bytes 4887596 | solution.py:215
  127.9 12.0 %conditional.6 = (bf16[4,32,384]{2,1,0:T(8,128)(2,1)S(1)}, bf16[128,1536]{1,0:T(8,128)(2,1)S(1)}, bf16[128,384]{1,0:T(8,128)(2,1)S(1)}) conditional(s32[]{:T(128)} %convert_element_type.123, () %tuple.45, (f32[10,38,384]{2,1,0:T(8,128)}, f32[49,384]{1,0:T(8,128)S(1)}, bf16[4,32,384]{2,1,0:T(8,128)(2,1)S(1)}, s32[]{:T(128)}, f32[1,2,384]{2,1,0:T(2,128)}, ...), branch_computations={%region_8.9_spmd, %region_9.14_spmd} | conditional | flops 488964224 | bytes 9917570 | solution.py:200
  128.0 3.3 fusion.116
  140.0 4.0 %collective-permute-start.21 = (bf16[3,32,384]{2,1,0:T(8,128)(2,1)S(1)}, bf16[3,32,384]{2,1,0:T(8,128)(2,1)S(1)}, u32[]{:S(2)}, u32[]{:S(2)}) collective-permute-start(bf16[3,32,384]{2,1,0:T(8,128)(2,1)S(1)} %get-tuple-element.142), channel_id=1, source_target_pairs={{0,1},{1,2},{2,3},{3,4},{4,5},{5,6},{6,7},{7,8},{8,9},{9,10},{10,1... | collective-permute-start | bytes 221192 | tf_op jit(solution)/shard_map/ppermute | solution.py:36
  146.5 3.8 collective-permute-done.22
  150.3 4.3 %conditional.7 = (bf16[4,32,384]{2,1,0:T(8,128)(2,1)S(1)}, f32[49,384]{1,0:T(8,128)S(1)}) conditional(s32[]{:T(128)} %convert_element_type.123, () %tuple.40, (bf16[4,32,384]{2,1,0:T(8,128)(2,1)S(1)}, bf16[10,32,384]{2,1,0:T(8,128)(2,1)S(1)}, f32[49,384]{1,0:T(8,128)S(1)}, f32[10,38,384]{2,1,0:T(8,128)S(1)}, ...), branch_computations={%region_14.15_spmd, %region_15.16_spmd} | conditional | flops 57950208 | bytes 2552848 | solution.py:215
  159.5 100.2 %all-reduce.6.cloned.1.call-done = f32[49,384]{1,0:T(8,128)} async-done(((f32[49,384]{1,0:T(8,128)}), f32[49,384]{1,0:T(8,128)}) %all-reduce.6.cloned.1.call-update) | async-done | bytes 75280 | tf_op jit(solution)/shard_map/psum | solution.py:246
  261.3 131.4 %reduce-scatter.2.cloned.1.call-done = f32[96,384]{1,0:T(8,128)} async-done(((f32[1536,384]{1,0:T(8,128)}), f32[96,384]{1,0:T(8,128)}) %reduce-scatter.2.cloned.1.call-update) | async-done | bytes 147472 | tf_op jit(solution)/shard_map/reduce_scatter | solution.py:237
  (171 shorter events, 71.6 us)
Async XLA Ops:
  7.2 87.4 %all-gather.2.cloned.1.call-start = ((), (), s32[]{:S(2)}) async-start(), calls=%async_computation.1 | async-start | bytes 2506752 | tf_op jit(solution)/shard_map/all_gather | solution.py:150
  7.3 13.4 %collective-permute-start.2 = (bf16[1,2,24,1536]{3,2,1,0:T(8,128)(2,1)}, bf16[1,2,24,1536]{3,2,1,0:T(8,128)(2,1)}, u32[]{:S(2)}, u32[]{:S(2)}) collective-permute-start(bf16[1,2,24,1536]{3,2,1,0:T(8,128)(2,1)} %param.26), channel_id=1, source_target_pairs={{0,1},{1,2},{2,3},{3,4},{4,5},{5,6},{6,7},{7,8},{8,9},{9,10},{10,1... | collective-permute-start | bytes 442376 | tf_op jit(solution)/shard_map/ppermute | solution.py:18
  10.2 13.1 %collective-permute-start.3 = (bf16[1,2,24,1536]{3,2,1,0:T(8,128)(2,1)}, bf16[1,2,24,1536]{3,2,1,0:T(8,128)(2,1)S(1)}, u32[]{:S(2)}, u32[]{:S(2)}) collective-permute-start(bf16[1,2,24,1536]{3,2,1,0:T(8,128)(2,1)} %param.26), channel_id=1, source_target_pairs={{0,15},{1,0},{2,1},{3,2},{4,3},{5,4},{6,5},{7,6},{8,7},{9,8},{10,9... | collective-permute-start | bytes 442376 | tf_op jit(solution)/shard_map/ppermute | solution.py:21
  16.9 9.8 %collective-permute-start = (bf16[2,3,32,384]{3,2,1,0:T(8,128)(2,1)}, bf16[2,3,32,384]{3,2,1,0:T(8,128)(2,1)S(1)}, u32[]{:S(2)}, u32[]{:S(2)}) collective-permute-start(bf16[2,3,32,384]{3,2,1,0:T(8,128)(2,1)} %get-tuple-element.140), channel_id=1, source_target_pairs={{0,1},{1,2},{2,3},{3,4},{4,5},{5,6},{6,7},{7,8},{8,9},{9,10},{10,1... | collective-permute-start | bytes 442376 | tf_op jit(solution)/shard_map/ppermute | solution.py:36
  18.2 8.5 %collective-permute-start.1 = (bf16[2,3,32,384]{3,2,1,0:T(8,128)(2,1)}, bf16[2,3,32,384]{3,2,1,0:T(8,128)(2,1)}, u32[]{:S(2)}, u32[]{:S(2)}) collective-permute-start(bf16[2,3,32,384]{3,2,1,0:T(8,128)(2,1)} %get-tuple-element.141), channel_id=1, source_target_pairs={{1,0},{2,1},{3,2},{4,3},{5,4},{6,5},{7,6},{8,7},{9,8},{10,9},{11,1... | collective-permute-start | bytes 442376 | tf_op jit(solution)/shard_map/ppermute | solution.py:38
  19.5 240.3 %all-reduce.6.cloned.1.call-start = ((), (), s32[]{:S(2)}) async-start(), calls=%async_computation.3 | async-start | bytes 172032 | tf_op jit(solution)/shard_map/psum | solution.py:246
  20.6 12.8 %collective-permute-start.4 = (bf16[1,2,24,1536]{3,2,1,0:T(8,128)(2,1)}, bf16[1,2,24,1536]{3,2,1,0:T(8,128)(2,1)S(1)}, u32[]{:S(2)}, u32[]{:S(2)}) collective-permute-start(bf16[1,2,24,1536]{3,2,1,0:T(8,128)(2,1)} %collective-permute-done.2), channel_id=1, source_target_pairs={{0,1},{1,2},{2,3},{3,4},{4,5},{5,6},{6,7},{7,8},{8,9},{9,10},{10,1... | collective-permute-start | bytes 442376 | tf_op jit(solution)/shard_map/ppermute | solution.py:18
  23.3 12.5 %collective-permute-start.5 = (bf16[1,2,24,1536]{3,2,1,0:T(8,128)(2,1)S(1)}, bf16[1,2,24,1536]{3,2,1,0:T(8,128)(2,1)S(1)}, u32[]{:S(2)}, u32[]{:S(2)}) collective-permute-start(bf16[1,2,24,1536]{3,2,1,0:T(8,128)(2,1)S(1)} %collective-permute-done.3), channel_id=1, source_target_pairs={{0,15},{1,0},{2,1},{3,2},{4,3},{5,4},{6,5},{7,6},{8,7},{9,8},{10,9... | collective-permute-start | bytes 442376 | tf_op jit(solution)/shard_map/ppermute | solution.py:21
  33.4 9.5 %collective-permute-start.6 = (bf16[1,2,24,1536]{3,2,1,0:T(8,128)(2,1)S(1)}, bf16[1,2,24,1536]{3,2,1,0:T(8,128)(2,1)S(1)}, u32[]{:S(2)}, u32[]{:S(2)}) collective-permute-start(bf16[1,2,24,1536]{3,2,1,0:T(8,128)(2,1)S(1)} %collective-permute-done.4), channel_id=1, source_target_pairs={{0,1},{1,2},{2,3},{3,4},{4,5},{5,6},{6,7},{7,8},{8,9},{9,10},{10,1... | collective-permute-start | bytes 442376 | tf_op jit(solution)/shard_map/ppermute | solution.py:18
  35.8 8.5 %collective-permute-start.7 = (bf16[1,2,24,1536]{3,2,1,0:T(8,128)(2,1)S(1)}, bf16[1,2,24,1536]{3,2,1,0:T(8,128)(2,1)S(1)}, u32[]{:S(2)}, u32[]{:S(2)}) collective-permute-start(bf16[1,2,24,1536]{3,2,1,0:T(8,128)(2,1)S(1)} %collective-permute-done.5), channel_id=1, source_target_pairs={{0,15},{1,0},{2,1},{3,2},{4,3},{5,4},{6,5},{7,6},{8,7},{9,8},{10,9... | collective-permute-start | bytes 442376 | tf_op jit(solution)/shard_map/ppermute | solution.py:21
  43.0 8.9 %collective-permute-start.8 = (bf16[1,2,24,1536]{3,2,1,0:T(8,128)(2,1)S(1)}, bf16[1,2,24,1536]{3,2,1,0:T(8,128)(2,1)S(1)}, u32[]{:S(2)}, u32[]{:S(2)}) collective-permute-start(bf16[1,2,24,1536]{3,2,1,0:T(8,128)(2,1)S(1)} %collective-permute-done.6), channel_id=1, source_target_pairs={{0,1},{1,2},{2,3},{3,4},{4,5},{5,6},{6,7},{7,8},{8,9},{9,10},{10,1... | collective-permute-start | bytes 442376 | tf_op jit(solution)/shard_map/ppermute | solution.py:18
  44.3 7.8 %collective-permute-start.9 = (bf16[1,2,24,1536]{3,2,1,0:T(8,128)(2,1)S(1)}, bf16[1,2,24,1536]{3,2,1,0:T(8,128)(2,1)S(1)}, u32[]{:S(2)}, u32[]{:S(2)}) collective-permute-start(bf16[1,2,24,1536]{3,2,1,0:T(8,128)(2,1)S(1)} %collective-permute-done.7), channel_id=1, source_target_pairs={{0,15},{1,0},{2,1},{3,2},{4,3},{5,4},{6,5},{7,6},{8,7},{9,8},{10,9... | collective-permute-start | bytes 442376 | tf_op jit(solution)/shard_map/ppermute | solution.py:21
  51.9 9.4 %collective-permute-start.10 = (bf16[1,2,24,1536]{3,2,1,0:T(8,128)(2,1)S(1)}, bf16[1,2,24,1536]{3,2,1,0:T(8,128)(2,1)S(1)}, u32[]{:S(2)}, u32[]{:S(2)}) collective-permute-start(bf16[1,2,24,1536]{3,2,1,0:T(8,128)(2,1)S(1)} %collective-permute-done.8), channel_id=1, source_target_pairs={{0,1},{1,2},{2,3},{3,4},{4,5},{5,6},{6,7},{7,8},{8,9},{9,10},{10,1... | collective-permute-start | bytes 442376 | tf_op jit(solution)/shard_map/ppermute | solution.py:18
  52.1 10.7 %collective-permute-start.11 = (bf16[1,2,24,1536]{3,2,1,0:T(8,128)(2,1)S(1)}, bf16[1,2,24,1536]{3,2,1,0:T(8,128)(2,1)S(1)}, u32[]{:S(2)}, u32[]{:S(2)}) collective-permute-start(bf16[1,2,24,1536]{3,2,1,0:T(8,128)(2,1)S(1)} %collective-permute-done.9), channel_id=1, source_target_pairs={{0,15},{1,0},{2,1},{3,2},{4,3},{5,4},{6,5},{7,6},{8,7},{9,8},{10,9... | collective-permute-start | bytes 442376 | tf_op jit(solution)/shard_map/ppermute | solution.py:21
  61.3 8.8 %collective-permute-start.12 = (bf16[1,2,24,1536]{3,2,1,0:T(8,128)(2,1)S(1)}, bf16[1,2,24,1536]{3,2,1,0:T(8,128)(2,1)S(1)}, u32[]{:S(2)}, u32[]{:S(2)}) collective-permute-start(bf16[1,2,24,1536]{3,2,1,0:T(8,128)(2,1)S(1)} %collective-permute-done.10), channel_id=1, source_target_pairs={{0,1},{1,2},{2,3},{3,4},{4,5},{5,6},{6,7},{7,8},{8,9},{9,10},{10,1... | collective-permute-start | bytes 442376 | tf_op jit(solution)/shard_map/ppermute | solution.py:18
  62.8 8.7 %collective-permute-start.13 = (bf16[1,2,24,1536]{3,2,1,0:T(8,128)(2,1)S(1)}, bf16[1,2,24,1536]{3,2,1,0:T(8,128)(2,1)S(1)}, u32[]{:S(2)}, u32[]{:S(2)}) collective-permute-start(bf16[1,2,24,1536]{3,2,1,0:T(8,128)(2,1)S(1)} %collective-permute-done.11), channel_id=1, source_target_pairs={{0,15},{1,0},{2,1},{3,2},{4,3},{5,4},{6,5},{7,6},{8,7},{9,8},{10,9... | collective-permute-start | bytes 442376 | tf_op jit(solution)/shard_map/ppermute | solution.py:21
  70.1 11.9 %collective-permute-start.14 = (bf16[1,2,24,1536]{3,2,1,0:T(8,128)(2,1)S(1)}, bf16[1,2,24,1536]{3,2,1,0:T(8,128)(2,1)S(1)}, u32[]{:S(2)}, u32[]{:S(2)}) collective-permute-start(bf16[1,2,24,1536]{3,2,1,0:T(8,128)(2,1)S(1)} %collective-permute-done.12), channel_id=1, source_target_pairs={{0,1},{1,2},{2,3},{3,4},{4,5},{5,6},{6,7},{7,8},{8,9},{9,10},{10,1... | collective-permute-start | bytes 442376 | tf_op jit(solution)/shard_map/ppermute | solution.py:18
  71.5 10.5 %collective-permute-start.15 = (bf16[1,2,24,1536]{3,2,1,0:T(8,128)(2,1)S(1)}, bf16[1,2,24,1536]{3,2,1,0:T(8,128)(2,1)S(1)}, u32[]{:S(2)}, u32[]{:S(2)}) collective-permute-start(bf16[1,2,24,1536]{3,2,1,0:T(8,128)(2,1)S(1)} %collective-permute-done.13), channel_id=1, source_target_pairs={{0,15},{1,0},{2,1},{3,2},{4,3},{5,4},{6,5},{7,6},{8,7},{9,8},{10,9... | collective-permute-start | bytes 442376 | tf_op jit(solution)/shard_map/ppermute | solution.py:21
  82.0 9.9 %collective-permute-start.16 = (bf16[1,2,24,1536]{3,2,1,0:T(8,128)(2,1)S(1)}, bf16[1,2,24,1536]{3,2,1,0:T(8,128)(2,1)S(1)}, u32[]{:S(2)}, u32[]{:S(2)}) collective-permute-start(bf16[1,2,24,1536]{3,2,1,0:T(8,128)(2,1)S(1)} %collective-permute-done.14), channel_id=1, source_target_pairs={{0,1},{1,2},{2,3},{3,4},{4,5},{5,6},{6,7},{7,8},{8,9},{9,10},{10,1... | collective-permute-start | bytes 442376 | tf_op jit(solution)/shard_map/ppermute | solution.py:18
  105.9 6.6 %collective-permute-start.17 = (bf16[3,32,384]{2,1,0:T(8,128)(2,1)S(1)}, bf16[3,32,384]{2,1,0:T(8,128)(2,1)S(1)}, u32[]{:S(2)}, u32[]{:S(2)}) collective-permute-start(bf16[3,32,384]{2,1,0:T(8,128)(2,1)S(1)} %get-tuple-element.144), channel_id=1, source_target_pairs={{0,1},{1,2},{2,3},{3,4},{4,5},{5,6},{6,7},{7,8},{8,9},{9,10},{10,1... | collective-permute-start | bytes 221192 | tf_op jit(solution)/shard_map/ppermute | solution.py:36
  110.3 6.2 %collective-permute-start.18 = (bf16[3,32,384]{2,1,0:T(8,128)(2,1)S(1)}, bf16[3,32,384]{2,1,0:T(8,128)(2,1)S(1)}, u32[]{:S(2)}, u32[]{:S(2)}) collective-permute-start(bf16[3,32,384]{2,1,0:T(8,128)(2,1)S(1)} %get-tuple-element.145), channel_id=1, source_target_pairs={{1,0},{2,1},{3,2},{4,3},{5,4},{6,5},{7,6},{8,7},{9,8},{10,9},{11,1... | collective-permute-start | bytes 221192 | tf_op jit(solution)/shard_map/ppermute | solution.py:38
  140.0 6.5 %collective-permute-start.21 = (bf16[3,32,384]{2,1,0:T(8,128)(2,1)S(1)}, bf16[3,32,384]{2,1,0:T(8,128)(2,1)S(1)}, u32[]{:S(2)}, u32[]{:S(2)}) collective-permute-start(bf16[3,32,384]{2,1,0:T(8,128)(2,1)S(1)} %get-tuple-element.142), channel_id=1, source_target_pairs={{0,1},{1,2},{2,3},{3,4},{4,5},{5,6},{6,7},{7,8},{8,9},{9,10},{10,1... | collective-permute-start | bytes 221192 | tf_op jit(solution)/shard_map/ppermute | solution.py:36
  146.4 10.3 %collective-permute-start.23 = (bf16[128,1920]{1,0:T(8,128)(2,1)S(1)}, bf16[128,1920]{1,0:T(8,128)(2,1)S(1)}, u32[]{:S(2)}, u32[]{:S(2)}) collective-permute-start(bf16[128,1920]{1,0:T(8,128)(2,1)S(1)} %pad_maximum_fusion.1), channel_id=1, source_target_pairs={{0,16},{16,0},{1,17},{17,1},{2,18},{18,2},{3,19},{19,3},{4,20},{20... | collective-permute-start | bytes 1474568 | tf_op jit(solution)/shard_map/ppermute | solution.py:62
  156.6 236.2 %reduce-scatter.2.cloned.1.call-start = ((), (), s32[]{:S(2)}) async-start(), calls=%async_computation.2 | async-start | bytes 2506752 | tf_op jit(solution)/shard_map/reduce_scatter | solution.py:237
  (22 other events, 444.7 us)
Sparse Core Ops, SparseCore 0:
  19.6 74.9 all-gather.1
  156.7 102.9 all-reduce.5
  265.2 127.4 reduce-scatter.1
